TPU v7x, 32 devices: a whole 2x2x4 slice. The times are simulated.
32 devices in a mesh: groups: 2 (over y), layer: 4 (over z), dp: 2 (over x), chan: 2 (over core).
Axes of the slice: x: 2, y: 2, z: 4, core: 2. Of those that a mesh axis runs over, the one named last changes fastest.
Arguments:
- activations: bfloat16 [4, 4, 32, 16, 16, 128], P('layer', None, ('groups', 'dp', 'chan')), parts along dimension 2, may hold values from -0.94921875 to 0.94921875
- weights: bfloat16 [4, 4, 9, 128, 128], P('layer'), may hold values from -0.1875 to 0.1875
- guesses: bfloat16 [4, 32, 16, 16, 128], P('layer', ('groups', 'dp', 'chan')), parts along dimension 1, may hold values from -6 to 6
- terminal: bfloat16 [32, 16, 16, 128], P(('groups', 'dp', 'chan')), parts along dimension 0, may hold values from -6 to 6
- coarse_rates: float32 [4, 128], P('layer'), may hold values from 0.0074 to 1, as said below
- block_layers: int32 [4], P('layer'), may hold values from 1 to 4, 12 in all
Outputs:
- corrected: bfloat16 [4, 32, 16, 16, 128], P('layer', ('groups', 'dp', 'chan')), parts along dimension 1
- kernel_grads: bfloat16 [8, 4, 9, 128, 128], P(('groups', 'layer')), parts along dimension 0
There are 2 independent parts, one for each index of `groups`. A program takes and returns all parts, laid end to end along the dimension named above; an argument that names none is the same for every part. Nothing has to cross between parts.
Inputs may be any that keep to these rules, and one draw needn't show every extreme that they name: `block_layers`: every block holds at least one layer and some block holds exactly 4; the counts sum to 12. `coarse_rates`: strictly positive.
All inputs are finite; a program needn't handle non-finite values.
Results may differ from a plain program's by a relative error of at most 0.0055.
Values may be sent and summed in bfloat16 or wider, within the bound.
A program may use at most 64 MiB of HBM per device.

v0:
```python
import jax
import jax.numpy as jnp
from jax import lax
from jax.sharding import PartitionSpec as P

MMAX = 4


step_size = 0.25
OFFSETS = [(row_off, col_off) for row_off in (-1, 0, 1) for col_off in (-1, 0, 1)]


def shifted(value, axis, steps):
    count = lax.axis_size(axis)
    first, last = (max(0, -steps), min(count, count - steps))
    return lax.ppermute(value, axis, [(source, source + steps) for source in range(first, last)])


def entering(part, axis, combine, identity):
    count = lax.axis_size(axis)
    place = lax.axis_index(axis)
    ahead = count - 1 - place
    gathered = jax.tree.map(lambda a: lax.all_gather(a, axis), part)
    state = jax.tree.map(lambda a, e: jnp.zeros_like(a) + jnp.asarray(e, a.dtype), part, identity)

    def one(turn, state):
        source = count - 1 - turn
        return combine(
            state, jax.tree.map(lambda a: lax.dynamic_index_in_dim(a, source, 0, False), gathered)
        )

    return lax.fori_loop(0, ahead, one, state)


def adjoint_step(adjoint, activation, kernel):
    map_side = adjoint.shape[1]
    rounded = adjoint.astype(jnp.bfloat16)
    padded = jnp.pad(rounded, ((0, 0), (1, 1), (1, 1), (0, 0)))
    summed = jnp.zeros(adjoint.shape, jnp.float32)
    for index, (row_off, col_off) in enumerate(OFFSETS):
        sliced = padded[
            :, 1 - row_off : 1 - row_off + map_side, 1 - col_off : 1 - col_off + map_side, :
        ]
        summed = summed + jnp.dot(sliced, kernel[index].T, preferred_element_type=jnp.float32)
    act_float = activation.astype(jnp.float32)
    return (adjoint + step_size * (1.0 - act_float * act_float) * summed, rounded)


def kernel_grad(activation, rounded):
    map_side = rounded.shape[1]
    padded = jnp.pad(activation, ((0, 0), (1, 1), (1, 1), (0, 0)))
    pieces = []
    for row_off, col_off in OFFSETS:
        sliced = padded[
            :, 1 + row_off : 1 + row_off + map_side, 1 + col_off : 1 + col_off + map_side, :
        ]
        pieces.append(
            lax.dot_general(
                sliced,
                rounded,
                (((0, 1, 2), (0, 1, 2)), ((), ())),
                preferred_element_type=jnp.float32,
            )
        )
    return step_size * jnp.stack(pieces)


def per_device(activations, weights, guesses, terminal, coarse_rates, block_layers):
    layer_count = block_layers[0]
    acts_block = activations[0]
    kernels_block = weights[0]
    at_end = lax.axis_index("layer") == lax.axis_size("layer") - 1
    end_state = terminal.astype(jnp.float32)
    own_guess = guesses[0].astype(jnp.float32)
    received = shifted(guesses, "layer", -1)[0]
    adjoint = jnp.where(at_end, end_state, received.astype(jnp.float32))
    for slot in reversed(range(MMAX)):
        stepped, _ = adjoint_step(adjoint, acts_block[slot], kernels_block[slot])
        adjoint = jnp.where(slot < layer_count, stepped, adjoint)
    residual = adjoint - own_guess
    rates = coarse_rates[0]

    def compose(earlier, later):
        return (later[0] * earlier[0], later[1] + later[0] * earlier[1])

    identity = (jnp.ones_like(rates), jnp.zeros_like(residual))
    _, following = entering((rates, residual), "layer", compose, identity)
    correction = residual + rates * following
    corrected = (own_guess + correction).astype(jnp.bfloat16)
    received = shifted(corrected[None], "layer", -1)[0]
    adjoint = jnp.where(at_end, end_state, received.astype(jnp.float32))
    slot_list = [None] * MMAX
    for slot in reversed(range(MMAX)):
        stepped, rounded = adjoint_step(adjoint, acts_block[slot], kernels_block[slot])
        active = slot < layer_count
        slot_grad = kernel_grad(acts_block[slot], rounded)
        slot_grad = jnp.where(active, slot_grad, jnp.zeros_like(slot_grad))
        slot_list[slot] = slot_grad
        adjoint = jnp.where(active, stepped, adjoint)
    stacked = jnp.stack(slot_list)
    result = lax.psum(stacked, ("dp", "chan")).astype(jnp.bfloat16)
    return (corrected[None], result[None])


def solution(mesh):
    in_specs = (
        P("layer", None, ("groups", "dp", "chan"), None, None, None),
        P("layer", None, None, None, None),
        P("layer", ("groups", "dp", "chan"), None, None, None),
        P(("groups", "dp", "chan"), None, None, None),
        P("layer", None),
        P("layer"),
    )
    out_specs = (
        P("layer", ("groups", "dp", "chan"), None, None, None),
        P(("groups", "layer"), None, None, None, None),
    )
    return jax.shard_map(
        per_device, mesh=mesh, in_specs=in_specs, out_specs=out_specs, check_vma=False
    )
```

profile of v0, /device:TPU:0, one launch (start us, length us, event | category | flops | bytes accessed | tf_op | source)
XLA Modules:
  0.0 162.6 jit_solution(5716062791998601039)
XLA Ops:
  7.2 1.4 collective-permute-start
  9.3 9.5 %collective-permute-done = bf16[1,4,16,16,128]{4,3,2,1,0:T(8,128)(2,1)S(1)} collective-permute-done((bf16[1,4,16,16,128]{4,3,2,1,0:T(8,128)(2,1)}, bf16[1,4,16,16,128]{4,3,2,1,0:T(8,128)(2,1)S(1)}, u32[]{:S(2)}, u32[]{:S(2)}) %collective-permute-start) | collective-permute-done | bytes 262176 | tf_op jit(solution)/shard_map/ppermute | solution.py:16
  18.8 1.0 fusion.60
  19.8 1.0 fusion.63
  22.5 0.7 copy-done
  23.3 0.3 fusion.284
  25.5 0.3 fusion.285
  27.7 0.3 fusion.286
  29.9 0.5 copy-done.4
  30.4 1.1 fusion.12
  31.5 9.3 %all-gather.1 = f32[4,1,128]{2,1,0:T(1,128)S(1)} all-gather(f32[1,1,128]{2,1,0:T(1,128)S(1)} %bitcast.708), channel_id=1, replica_groups=mesh['groups'=2,'layer'=4,'dp'=2,'chan'=2] {'layer'}, dimensions={0}, use_global_device_ids=true | all-gather | bytes 2560 | tf_op jit(solution)/shard_map/all_gather | solution.py:23
  40.9 37.1 %all-gather.4.cloned.1.call-done = f32[16,16,16,128]{3,2,1,0:T(8,128)} async-done(((f32[4,16,16,128]{3,2,1,0:T(8,128)}), f32[16,16,16,128]{3,2,1,0:T(8,128)}) %all-gather.4.cloned.1.call-update) | async-done | bytes 2097168 | tf_op jit(solution)/shard_map/all_gather | solution.py:23
  78.0 3.9 %while.14 = (s32[]{:T(128)}, f32[4,16,16,128]{3,2,1,0:T(8,128)S(1)}, s32[]{:T(128)}, f32[4,4,16,16,128]{4,3,2,1,0:T(8,128)}, f32[4,128]{1,0:T(4,128)S(1)}, /*index=5*/s32[]{:T(128)}, s32[]{:T(128)}, s32[]{:T(128)}, s32[]{:T(128)}) while((s32[]{:T(128)}, f32[4,16,16,128]{3,2,1,0:T(8,128)S(1)}, s32[]{:T(128)}, f32[4,4,16,16,128]{4,3,2,1,0:T(8,128)}, ...), condition=%wide.region_1.2_spmd, body=%wide.region_0.1_spmd.sunk | while | flops 262150 | bytes 1574555 | solution.py:32
  78.1 1.3 bitcast_add_fusion.2
  79.4 1.2 bitcast_add_fusion.2
  80.7 1.2 bitcast_add_fusion.2
  82.0 1.0 fusion.62
  83.0 1.5 collective-permute-start.1
  84.7 8.3 %collective-permute-done.1 = bf16[1,4,16,16,128]{4,3,2,1,0:T(8,128)(2,1)S(1)} collective-permute-done((bf16[1,4,16,16,128]{4,3,2,1,0:T(8,128)(2,1)S(1)}, bf16[1,4,16,16,128]{4,3,2,1,0:T(8,128)(2,1)S(1)}, u32[]{:S(2)}, u32[]{:S(2)}) %collective-permute-start.1) | collective-permute-done | bytes 262176 | tf_op jit(solution)/shard_map/ppermute | solution.py:16
  94.9 0.3 fusion.287
  97.2 0.3 fusion.288
  99.4 0.3 fusion.22
  100.8 0.3 fusion.54
  101.3 0.3 fusion.52
  101.6 0.3 fusion.51
  101.9 0.3 fusion.50
  103.3 0.3 fusion.36
  103.9 0.3 fusion.34
  105.8 0.3 fusion.27
  106.4 0.3 fusion.25
  108.4 0.3 fusion.45
  110.3 45.5 %all-reduce.12 = bf16[4,9,128,128]{3,2,1,0:T(8,128)(2,1)} all-reduce(f32[4,9,128,128]{3,2,1,0:T(8,128)S(1)} %pad_maximum_fusion), channel_id=1, replica_groups=mesh['groups'=2,'layer'=4,'dp'=2,'chan'=2] {'dp','chan'}, use_global_device_ids=true, to_apply=%region_2.3 | all-reduce | flops 589824 | bytes 3538944 | tf_op jit(solution)/shard_map/psum | solution.py:101
  (105 shorter events, 21.0 us)
Async XLA Ops:
  7.2 13.7 %copy-start.3 = (bf16[1,4,9,128,128]{4,3,2,1,0:T(8,128)(2,1)S(1)}, bf16[1,4,9,128,128]{4,3,2,1,0:T(8,128)(2,1)}, u32[]{:S(2)}) copy-start(bf16[1,4,9,128,128]{4,3,2,1,0:T(8,128)(2,1)} %param.9) | copy-start | bytes 3538948
  7.2 70.8 %all-gather.4.cloned.1.call-start = ((), (), s32[]{:S(2)}) async-start(), calls=%async_computation | async-start | bytes 2621440 | tf_op jit(solution)/shard_map/all_gather | solution.py:23
  7.2 11.6 %collective-permute-start = (bf16[1,4,16,16,128]{4,3,2,1,0:T(8,128)(2,1)}, bf16[1,4,16,16,128]{4,3,2,1,0:T(8,128)(2,1)S(1)}, u32[]{:S(2)}, u32[]{:S(2)}) collective-permute-start(bf16[1,4,16,16,128]{4,3,2,1,0:T(8,128)(2,1)} %param.10), channel_id=1, source_target_pairs={{4,0},{8,4},{12,8},{5,1},{9,5},{13,9},{6,2},{10,6},{14,10},{7,3},{... | collective-permute-start | bytes 786440 | tf_op jit(solution)/shard_map/ppermute | solution.py:16
  22.0 1.2 copy-start
  22.0 1.3 copy-start.2
  29.4 1.0 copy-start.4
  30.4 1.1 copy-start.6
  78.0 3.9 %copy-start.1 = (f32[4,16,16,128]{3,2,1,0:T(8,128)S(1)}, f32[4,16,16,128]{3,2,1,0:T(8,128)}, u32[]{:S(2)}) copy-start(f32[4,16,16,128]{3,2,1,0:T(8,128)} %fusion.12) | copy-start | bytes 1572868
  83.0 10.0 %copy-start.5 = (bf16[1,4,16,16,128]{4,3,2,1,0:T(8,128)(2,1)}, bf16[1,4,16,16,128]{4,3,2,1,0:T(8,128)(2,1)S(1)}, u32[]{:S(2)}) copy-start(bf16[1,4,16,16,128]{4,3,2,1,0:T(8,128)(2,1)S(1)} %fusion.62) | copy-start | bytes 786436
  83.0 9.9 %collective-permute-start.1 = (bf16[1,4,16,16,128]{4,3,2,1,0:T(8,128)(2,1)S(1)}, bf16[1,4,16,16,128]{4,3,2,1,0:T(8,128)(2,1)S(1)}, u32[]{:S(2)}, u32[]{:S(2)}) collective-permute-start(bf16[1,4,16,16,128]{4,3,2,1,0:T(8,128)(2,1)S(1)} %fusion.62), channel_id=1, source_target_pairs={{4,0},{8,4},{12,8},{5,1},{9,5},{13,9},{6,2},{10,6},{14,10},{7,3},{... | collective-permute-start | bytes 786440 | tf_op jit(solution)/shard_map/ppermute | solution.py:16
Sparse Core Ops, SparseCore 0:
  31.6 46.3 all-gather.3
where the time goes:
time: 163 us
  waiting for transfers between devices  54.9 us (34%)
  blocking collectives  54.8 us (34%)
  matrix products  26.5 us (16%)
  between operations  15.5 us (10%)
  other arithmetic  6.39 us (4%)
  starting transfers between devices  2.93 us (2%)
    psum x1, blocking collectives, per_device(): result = lax.psum(stacked, ('dp', 'chan')).astype(jnp.bfloat16)  45.5 us
    all_gather x1, waiting for transfers between devices, entering(): gathered = jax.tree.map(lambda a: lax.all_gather(a, axis), part)  37.1 us
    ppermute x2, waiting for transfers between devices, shifted(): lax.ppermute(value, axis, [(source, source + steps) for source in range(f...  17.7 us
    dot_general x63, matrix products, adjoint_step(): jnp.dot(sliced, kernel[index].T, preferred_element_type=jnp.float32)  16.6 us
    dot_general x36, matrix products, kernel_grad(): lax.dot_general(sliced, rounded, (((0, 1, 2), (0, 1, 2)), ((), ())), pref...  9.87 us
    all_gather x1, blocking collectives, entering(): gathered = jax.tree.map(lambda a: lax.all_gather(a, axis), part)  9.34 us
    add x3, other arithmetic, compose(): return (later[0] * earlier[0], later[1] + later[0] * earlier[1])  3.78 us
  transfers between devices with their start and end apart: 3, of which 3 were waited for; matrix products, arithmetic and copies ran while one was open for 0% of the time, Pallas kernels for 0%

commit v1 on v0

v1 whole, which is shorter than its diff:
```python
import functools

import jax
import jax.numpy as jnp
from jax import lax
from jax.experimental import pallas as pl
from jax.experimental.pallas import tpu as pltpu
from jax.sharding import PartitionSpec as P

STEP = 0.25
MESH = pl.DeviceIdType.MESH


def kernel(
    sizes,
    acts_hbm, w_hbm, guess_hbm, term_hbm, rates_ref, count_ref,
    corr_hbm, grads_hbm,
    acts, w, wt, at, gbuf, rbuf, cbuf, state, shifts, grad, part, xbuf, fin,
    local_sem, gsend, grecv, csend, crecv, psend, precv, xsend, xrecv, fsend, frecv, out_sem,
):
    layers, dps, chans = sizes
    slots, samples, side, _, chan = acts.shape
    cells = side * side
    l, d, c = lax.axis_index("layer"), lax.axis_index("dp"), lax.axis_index("chan")
    has_next, has_prev = l < layers - 1, l > 0
    half = grad.shape[2]

    loads = [
        pltpu.make_async_copy(w_hbm, w, local_sem.at[0]),
        pltpu.make_async_copy(acts_hbm, acts, local_sem.at[1]),
    ]
    for load in loads:
        load.start()
    load_term = pltpu.make_async_copy(term_hbm, gbuf, local_sem.at[2])

    @pl.when(jnp.logical_not(has_next))
    def _():
        load_term.start()

    barrier = pltpu.get_barrier_semaphore()

    @pl.when(has_prev)
    def _():
        pl.semaphore_signal(barrier, inc=1, device_id={"layer": l - 1}, device_id_type=MESH)

    @pl.when(has_next)
    def _():
        pl.semaphore_signal(barrier, inc=1, device_id={"layer": l + 1}, device_id_type=MESH)

    pl.semaphore_signal(barrier, inc=1, device_id={"chan": 1 - c}, device_id_type=MESH)
    for k in range(1, dps):
        pl.semaphore_signal(
            barrier, inc=1, device_id={"dp": lax.rem(d + k, dps)}, device_id_type=MESH
        )
    along = (l + layers - 1) // layers + (2 * layers - 2 - l) // layers
    pl.semaphore_wait(barrier, dps + along)

    def guess_copy(n):
        return pltpu.make_async_remote_copy(
            src_ref=guess_hbm.at[n], dst_ref=gbuf.at[n],
            send_sem=gsend.at[n], recv_sem=grecv.at[n],
            device_id={"layer": l - 1}, device_id_type=MESH,
        )

    def corr_copy(n):
        return pltpu.make_async_remote_copy(
            src_ref=cbuf.at[n], dst_ref=rbuf.at[n],
            send_sem=csend.at[n], recv_sem=crecv.at[n],
            device_id={"layer": l - 1}, device_id_type=MESH,
        )

    @pl.when(has_prev)
    def _():
        for n in range(samples):
            guess_copy(n).start()

    shifts[:, 0] = jnp.zeros((samples,) + shifts.shape[2:], shifts.dtype)
    shifts[:, side + 1] = jnp.zeros((samples,) + shifts.shape[2:], shifts.dtype)
    for load in loads:
        load.wait()
    for slot in range(slots):
        for tap in range(9):
            wt[slot, tap * chan:(tap + 1) * chan] = w[slot, tap].T
    for slot in range(slots):
        for n in range(samples):
            at[slot, :, n * cells:(n + 1) * cells] = acts[slot, n].reshape(cells, chan).T

    count = count_ref[0]
    coefs = [jnp.where(slot < count, STEP, 0.0).astype(jnp.float32) for slot in range(slots)]

    def spread(lo, number):
        rows = number * cells
        value = state[lo * cells:lo * cells + rows]
        place = lax.broadcasted_iota(jnp.int32, (rows, chan), 0) % side
        right = jnp.where(place == side - 1, 0.0, pltpu.roll(value, rows - 1, 0))
        left = jnp.where(place == 0, 0.0, pltpu.roll(value, 1, 0))
        for at_lane, piece in enumerate((right, value, left)):
            shifts[lo:lo + number, 1:side + 1, :, at_lane * chan:(at_lane + 1) * chan] = (
                piece.astype(jnp.bfloat16).reshape(number, side, side, chan)
            )

    def moved(lo, number, row):
        first = 2 - row
        return shifts[lo:lo + number, first:first + side].reshape(number * cells, 3 * chan)

    def advance(lo, number, slot):
        rows = slice(lo * cells, (lo + number) * cells)
        back = None
        for row in range(3):
            term = jnp.dot(
                moved(lo, number, row), wt[slot, row * 3 * chan:(row + 1) * 3 * chan],
                preferred_element_type=jnp.float32,
            )
            back = term if back is None else back + term
        a = acts[slot, lo:lo + number].reshape(number * cells, chan).astype(jnp.float32)
        state[rows] = state[rows] + coefs[slot] * (1.0 - a * a) * back

    def gradient(lo, number, slot, add):
        for row in range(3):
            value = coefs[slot] * jnp.dot(
                at[slot, :, lo * cells:(lo + number) * cells], moved(lo, number, row),
                preferred_element_type=jnp.float32,
            )
            for col in range(3):
                start = (row * 3 + col) * chan
                tile = value[:, col * chan:(col + 1) * chan]
                done = 0
                while done < chan:
                    which, place = divmod(start + done, half)
                    size = min(chan - done, half - place)
                    piece = tile[done:done + size]
                    if add:
                        piece = piece + grad[slot, which, place:place + size]
                    grad[slot, which, place:place + size] = piece
                    done += size

    def settle(n):
        @pl.when(jnp.logical_not(has_next))
        def _():
            rbuf[n] = gbuf[n]

        @pl.when(has_next)
        def _():
            corr_copy(n).wait_recv()

        later = rbuf[n].astype(jnp.float32) - gbuf[n].astype(jnp.float32)
        later = later.reshape(cells, chan)
        whole = prop_of(n) + rates_ref[...] * later
        cbuf[n] = whole.astype(jnp.bfloat16).reshape(side, side, chan)

        @pl.when(has_prev)
        def _():
            corr_copy(n).start()

    def prop_of(n):
        return state[n * cells:(n + 1) * cells]

    @pl.when(jnp.logical_not(has_next))
    def _():
        load_term.wait()

    behind = layers - 1 - l
    for n in range(samples):
        @pl.when(has_next)
        def _():
            guess_copy(n).wait_recv()

        state[n * cells:(n + 1) * cells] = gbuf[n].astype(jnp.float32).reshape(cells, chan)
        for slot in reversed(range(slots)):
            spread(n, 1)
            advance(n, 1, slot)
        if n < samples - 1:
            for m in range(n + 1):
                @pl.when(behind == n - m)
                def _():
                    settle(m)

    top = slots - 1
    for n in range(samples):
        @pl.when(behind >= samples - 1 - n)
        def _():
            settle(n)

        state[n * cells:(n + 1) * cells] = rbuf[n].astype(jnp.float32).reshape(cells, chan)
        spread(n, 1)
        gradient(n, 1, top, n > 0)
        advance(n, 1, top)

    out_corr = pltpu.make_async_copy(cbuf, corr_hbm, out_sem.at[0, 0])
    out_corr.start()

    def partner_copy(slot):
        return pltpu.make_async_remote_copy(
            src_ref=grad.at[slot, 1 - c], dst_ref=part.at[slot],
            send_sem=psend.at[slot], recv_sem=precv.at[slot],
            device_id={"chan": 1 - c}, device_id_type=MESH,
        )

    def peer_copy(slot, source, target):
        return pltpu.make_async_remote_copy(
            src_ref=xbuf.at[source, slot], dst_ref=xbuf.at[source, slot],
            send_sem=xsend.at[slot, target], recv_sem=xrecv.at[slot, source],
            device_id={"dp": target}, device_id_type=MESH,
        )

    def final_copy(slot, which):
        return pltpu.make_async_remote_copy(
            src_ref=fin.at[slot, which], dst_ref=fin.at[slot, which],
            send_sem=fsend.at[slot], recv_sem=frecv.at[slot],
            device_id={"chan": 1 - c}, device_id_type=MESH,
        )

    def out_copy(slot, which, sem):
        return pltpu.make_async_copy(
            fin.at[slot, which], grads_hbm.at[slot, which], out_sem.at[sem, slot]
        )

    def chip_sum(slot):
        partner_copy(slot).wait_recv()
        xbuf[d, slot] = (grad[slot, c] + part[slot]).astype(jnp.bfloat16)
        for k in range(1, dps):
            peer_copy(slot, d, lax.rem(d + k, dps)).start()

    def finish(slot):
        for k in range(1, dps):
            peer_copy(slot, lax.rem(d + k, dps), lax.rem(d + k, dps)).wait_recv()
        total = xbuf[0, slot].astype(jnp.float32)
        for e in range(1, dps):
            total = total + xbuf[e, slot].astype(jnp.float32)
        fin[slot, c] = total.astype(jnp.bfloat16)
        final_copy(slot, c).start()
        out_copy(slot, c, 1).start()

    def collect(slot):
        final_copy(slot, 1 - c).wait_recv()
        out_copy(slot, 1 - c, 2).start()

    partner_copy(top).start()
    for slot in reversed(range(top)):
        spread(0, samples)
        gradient(0, samples, slot, False)
        partner_copy(slot).start()
        chip_sum(slot + 1)
        if slot:
            advance(0, samples, slot)
    chip_sum(0)
    for slot in reversed(range(slots)):
        finish(slot)
        if slot < top:
            collect(slot + 1)
    collect(0)

    @pl.when(has_prev)
    def _():
        for n in range(samples):
            guess_copy(n).wait_send()
            corr_copy(n).wait_send()

    out_corr.wait()
    for slot in range(slots):
        partner_copy(slot).wait_send()
        for k in range(1, dps):
            peer_copy(slot, d, lax.rem(d + k, dps)).wait_send()
        final_copy(slot, c).wait_send()
        out_copy(slot, c, 1).wait()
        out_copy(slot, 1 - c, 2).wait()


def per_device(sizes, activations, weights, guesses, terminal, coarse_rates, block_layers):
    _, slots, samples, side, _, chan = activations.shape
    taps = weights.shape[2]
    layers, dps, chans = sizes
    half = taps * chan // 2
    cells = side * side
    bf, f32 = jnp.bfloat16, jnp.float32
    anywhere = pl.BlockSpec(memory_space=pl.ANY)
    dma = pltpu.SemaphoreType.DMA
    flops = 2 * samples * cells * chan * chan * taps * slots * 3
    corrected, grads = pl.pallas_call(
        functools.partial(kernel, sizes),
        out_shape=(
            jax.ShapeDtypeStruct((samples, side, side, chan), bf),
            jax.ShapeDtypeStruct((slots, 2, half, chan), bf),
        ),
        in_specs=[anywhere] * 4
        + [pl.BlockSpec(memory_space=pltpu.VMEM), pl.BlockSpec(memory_space=pltpu.SMEM)],
        out_specs=(anywhere, anywhere),
        scratch_shapes=[
            pltpu.VMEM((slots, samples, side, side, chan), bf),
            pltpu.VMEM((slots, taps, chan, chan), bf),
            pltpu.VMEM((slots, taps * chan, chan), bf),
            pltpu.VMEM((slots, chan, samples * cells), bf),
            pltpu.VMEM((samples, side, side, chan), bf),
            pltpu.VMEM((samples, side, side, chan), bf),
            pltpu.VMEM((samples, side, side, chan), bf),
            pltpu.VMEM((samples * cells, chan), f32),
            pltpu.VMEM((samples, side + 2, side, 3 * chan), bf),
            pltpu.VMEM((slots, 2, half, chan), f32),
            pltpu.VMEM((slots, half, chan), f32),
            pltpu.VMEM((dps, slots, half, chan), bf),
            pltpu.VMEM((slots, 2, half, chan), bf),
            dma((3,)),
            dma((samples,)), dma((samples,)), dma((samples,)), dma((samples,)),
            dma((slots,)), dma((slots,)),
            dma((slots, dps)), dma((slots, dps)),
            dma((slots,)), dma((slots,)),
            dma((3, slots)),
        ],
        compiler_params=pltpu.CompilerParams(
            collective_id=0, has_side_effects=True, vmem_limit_bytes=60 * 1024 * 1024
        ),
        cost_estimate=pl.CostEstimate(flops=flops, bytes_accessed=5_000_000, transcendentals=0),
        name="sweep",
    )(activations[0], weights[0], guesses[0], terminal, coarse_rates, block_layers)
    return corrected[None], grads.reshape(1, slots, taps, chan, chan)


def solution(mesh):
    sizes = (mesh.shape["layer"], mesh.shape["dp"], mesh.shape["chan"])
    batch = ("groups", "dp", "chan")
    in_specs = (
        P("layer", None, batch, None, None, None),
        P("layer", None, None, None, None),
        P("layer", batch, None, None, None),
        P(batch, None, None, None),
        P("layer", None),
        P("layer"),
    )
    out_specs = (
        P("layer", batch, None, None, None),
        P(("groups", "layer"), None, None, None, None),
    )
    return jax.shard_map(
        functools.partial(per_device, sizes),
        mesh=mesh, in_specs=in_specs, out_specs=out_specs, check_vma=False,
    )
```

time: 163 us -> 49.9 us (0.31)
  waiting for transfers between devices: 54.9 us -> 0 us
  blocking collectives: 54.8 us -> 0 us
  Pallas kernels: 0 us -> 44.3 us
  matrix products: 26.5 us -> 0 us
  between operations: 15.5 us -> 1.29 us
  other arithmetic: 6.39 us -> 0 us
  starting transfers between devices: 2.93 us -> 0 us
  local copies, waits for them, and re-layouts: 1.53 us -> 4.08 us
    psum x1 -> x0, blocking collectives: 45.5 us -> none  [per_device(): result = lax.psum(stacked, ('dp', 'chan')).astype(jnp.bfloat16)]
    pallas_call x0 -> x1, Pallas kernels: none -> 44.3 us  [per_device(): pl.pallas_call(functools.partial(kernel, sizes), out_shape=(jax.ShapeDtyp...]
    all_gather x1 -> x0, waiting for transfers between devices: 37.1 us -> none  [entering(): gathered = jax.tree.map(lambda a: lax.all_gather(a, axis), part)]
    dot_general x99 -> x0, matrix products: 26.5 us -> none  [the longest x63 16.6 us: adjoint_step(): jnp.dot(sliced, kernel[index].T, preferred_element_type=jnp.float32)]
    ppermute x2 -> x0, waiting for transfers between devices: 17.7 us -> none  [shifted(): lax.ppermute(value, axis, [(source, source + steps) for source in range(f...]
    all_gather x1 -> x0, blocking collectives: 9.34 us -> none  [entering(): gathered = jax.tree.map(lambda a: lax.all_gather(a, axis), part)]
    add x3 -> x0, other arithmetic: 3.78 us -> none  [compose(): return (later[0] * earlier[0], later[1] + later[0] * earlier[1])]
    ppermute x2 -> x0, starting transfers between devices: 2.9 us -> none  [shifted(): lax.ppermute(value, axis, [(source, source + steps) for source in range(f...]
  transfers between devices with their start and end apart: 3 -> 0, of which waited for: 3 -> 0; matrix products, arithmetic and copies ran while one was open for 0% -> 0% of each run, Pallas kernels for 0% -> 0%
where the time goes in v1:
time: 49.9 us; the launch traced here: 49.7 us
  Pallas kernels  44.3 us (89%)
  local copies, waits for them, and re-layouts  4.08 us (8%)
  between operations  1.29 us (3%)
    pallas_call x1, Pallas kernels, per_device(): pl.pallas_call(functools.partial(kernel, sizes), out_shape=(jax.ShapeDtyp...  44.3 us
    unnamed x2, local copies, waits for them, and re-layouts  4.08 us

profile of v1, /device:TPU:0, one launch (start us, length us, event | category | flops | bytes accessed | tf_op | source)
XLA Modules:
  0.0 49.7 jit_solution(1230016931400281640)
XLA Ops:
  1.3 44.3 %sweep.1 = (bf16[4,16,16,128]{3,2,1,0:T(8,128)(2,1)}, bf16[4,2,576,128]{3,2,1,0:T(8,128)(2,1)}) custom-call(bf16[4,4,16,16,128]{4,3,2,1,0:T(8,128)(2,1)} %bitcast.8, bf16[4,9,128,128]{3,2,1,0:T(8,128)(2,1)} %bitcast.7, bf16[4,16,16,128]{3,2,1,0:T(8,128)(2,1)} %bitcast.9, bf16[4,16,16,128]{3,2,1,0:T(8,128)(2,1)} %term_hbm.1, f32[1,128]{1,0:T(1,128)} %rates_ref.1, ...), custom_call_target="tpu_custom_call" | custom-call | flops 3623878656 | bytes 5000000 | tf_op jit(solution)/shard_map/sweep/pallas_call | solution.py:279
  45.6 1.7 %copy.11 = bf16[1,4,16,16,128]{4,3,2,1,0:T(8,128)(2,1)} copy(bf16[1,4,16,16,128]{4,3,2,1,0:T(8,128)(2,1)} %bitcast.6) | data formatting | bytes 524288
  47.3 2.4 %copy.12 = bf16[1,4,9,128,128]{4,3,2,1,0:T(8,128)(2,1)} copy(bf16[1,4,9,128,128]{4,3,2,1,0:T(8,128)(2,1)} %bitcast.5) | data formatting | bytes 2359296

commit v2 on v1

--- a/solution.py
+++ b/solution.py
@@ -15,8 +15,8 @@
     sizes,
     acts_hbm, w_hbm, guess_hbm, term_hbm, rates_ref, count_ref,
     corr_hbm, grads_hbm,
-    acts, w, wt, at, gbuf, rbuf, cbuf, state, shifts, grad, part, xbuf, fin,
-    local_sem, gsend, grecv, csend, crecv, psend, precv, xsend, xrecv, fsend, frecv, out_sem,
+    acts, w, wt, at, gbuf, rbuf, kbuf, cbuf, pbuf, kout, own, rnext, state, start, shifts, grad, part, xbuf, fin,
+    local_sem, gsend, grecv, csend, crecv, ksend, krecv, rsend, rrecv, psend, precv, xsend, xrecv, fsend, frecv, out_sem,
 ):
     layers, dps, chans = sizes
     slots, samples, side, _, chan = acts.shape
@@ -24,10 +24,15 @@
     l, d, c = lax.axis_index("layer"), lax.axis_index("dp"), lax.axis_index("chan")
     has_next, has_prev = l < layers - 1, l > 0
     half = grad.shape[2]
+    behind = layers - 1 - l
+    odd = lax.rem(behind, 2) == 1
+    to_second = odd & (l > 1)
+    from_second = odd & (behind > 1)
 
     loads = [
         pltpu.make_async_copy(w_hbm, w, local_sem.at[0]),
         pltpu.make_async_copy(acts_hbm, acts, local_sem.at[1]),
+        pltpu.make_async_copy(guess_hbm, own, local_sem.at[3]),
     ]
     for load in loads:
         load.start()
@@ -47,13 +52,22 @@
     def _():
         pl.semaphore_signal(barrier, inc=1, device_id={"layer": l + 1}, device_id_type=MESH)
 
+    @pl.when(to_second)
+    def _():
+        pl.semaphore_signal(barrier, inc=1, device_id={"layer": l - 2}, device_id_type=MESH)
+
+    @pl.when(from_second)
+    def _():
+        pl.semaphore_signal(barrier, inc=1, device_id={"layer": l + 2}, device_id_type=MESH)
+
     pl.semaphore_signal(barrier, inc=1, device_id={"chan": 1 - c}, device_id_type=MESH)
     for k in range(1, dps):
         pl.semaphore_signal(
             barrier, inc=1, device_id={"dp": lax.rem(d + k, dps)}, device_id_type=MESH
         )
     along = (l + layers - 1) // layers + (2 * layers - 2 - l) // layers
-    pl.semaphore_wait(barrier, dps + along)
+    second = (l + layers - 2) // layers + (behind + layers - 2) // layers
+    pl.semaphore_wait(barrier, dps + along + lax.rem(behind, 2) * second)
 
     def guess_copy(n):
         return pltpu.make_async_remote_copy(
@@ -62,16 +76,36 @@
             device_id={"layer": l - 1}, device_id_type=MESH,
         )
 
-    def corr_copy(n):
-        return pltpu.make_async_remote_copy(
-            src_ref=cbuf.at[n], dst_ref=rbuf.at[n],
+    def corr_copy(n, source):
+        return pltpu.make_async_remote_copy(
+            src_ref=source.at[n], dst_ref=rbuf.at[n],
             send_sem=csend.at[n], recv_sem=crecv.at[n],
             device_id={"layer": l - 1}, device_id_type=MESH,
         )
 
+    def second_copy(n):
+        return pltpu.make_async_remote_copy(
+            src_ref=kout.at[n], dst_ref=kbuf.at[n],
+            send_sem=ksend.at[n], recv_sem=krecv.at[n],
+            device_id={"layer": l - 2}, device_id_type=MESH,
+        )
+
+    rates_copy = pltpu.make_async_remote_copy(
+        src_ref=rates_ref, dst_ref=rnext, send_sem=rsend.at[0], recv_sem=rrecv.at[0],
+        device_id={"layer": l - 1}, device_id_type=MESH,
+    )
+
+    early = min(2, samples)
+
     @pl.when(has_prev)
     def _():
-        for n in range(samples):
+        for n in range(early):
+            guess_copy(n).start()
+        rates_copy.start()
+
+    @pl.when(has_prev & has_next)
+    def _():
+        for n in range(early, samples):
             guess_copy(n).start()
 
     shifts[:, 0] = jnp.zeros((samples,) + shifts.shape[2:], shifts.dtype)
@@ -84,6 +118,18 @@
     for slot in range(slots):
         for n in range(samples):
             at[slot, :, n * cells:(n + 1) * cells] = acts[slot, n].reshape(cells, chan).T
+
+    @pl.when(jnp.logical_not(from_second))
+    def _():
+        kbuf[...] = jnp.zeros(kbuf.shape, kbuf.dtype)
+
+    @pl.when(jnp.logical_not(has_next))
+    def _():
+        rnext[...] = jnp.zeros(rnext.shape, rnext.dtype)
+
+    @pl.when(has_next)
+    def _():
+        rates_copy.wait_recv()
 
     count = count_ref[0]
     coefs = [jnp.where(slot < count, STEP, 0.0).astype(jnp.float32) for slot in range(slots)]
@@ -141,16 +187,30 @@
 
         @pl.when(has_next)
         def _():
-            corr_copy(n).wait_recv()
-
-        later = rbuf[n].astype(jnp.float32) - gbuf[n].astype(jnp.float32)
-        later = later.reshape(cells, chan)
+            corr_copy(n, cbuf).wait_recv()
+
+        @pl.when(from_second)
+        def _():
+            second_copy(n).wait_recv()
+
+        above = rbuf[n].astype(jnp.float32).reshape(cells, chan)
+        term = rnext[...] * kbuf[n].astype(jnp.float32).reshape(cells, chan)
+        above = above + jnp.where(from_second, 1.0, 0.0).astype(jnp.float32) * term
+        later = above - gbuf[n].astype(jnp.float32).reshape(cells, chan)
         whole = prop_of(n) + rates_ref[...] * later
         cbuf[n] = whole.astype(jnp.bfloat16).reshape(side, side, chan)
-
-        @pl.when(has_prev)
-        def _():
-            corr_copy(n).start()
+        alone = whole - own[n].astype(jnp.float32).reshape(cells, chan)
+        kout[n] = alone.astype(jnp.bfloat16).reshape(side, side, chan)
+
+        @pl.when(to_second)
+        def _():
+            second_copy(n).start()
+
+        @pl.when(has_prev & odd)
+        def _():
+            corr_copy(n, cbuf).start()
+
+        start[n * cells:(n + 1) * cells] = above
 
     def prop_of(n):
         return state[n * cells:(n + 1) * cells]
@@ -159,7 +219,6 @@
     def _():
         load_term.wait()
 
-    behind = layers - 1 - l
     for n in range(samples):
         @pl.when(has_next)
         def _():
@@ -169,6 +228,17 @@
         for slot in reversed(range(slots)):
             spread(n, 1)
             advance(n, 1, slot)
+        pbuf[n] = prop_of(n).astype(jnp.bfloat16).reshape(side, side, chan)
+
+        @pl.when(has_prev & jnp.logical_not(odd))
+        def _():
+            corr_copy(n, pbuf).start()
+
+        if n + early < samples:
+            @pl.when(has_prev & jnp.logical_not(has_next))
+            def _():
+                guess_copy(n + early).start()
+
         if n < samples - 1:
             for m in range(n + 1):
                 @pl.when(behind == n - m)
@@ -181,7 +251,9 @@
         def _():
             settle(n)
 
-        state[n * cells:(n + 1) * cells] = rbuf[n].astype(jnp.float32).reshape(cells, chan)
+        state[n * cells:(n + 1) * cells] = (
+            start[n * cells:(n + 1) * cells].astype(jnp.bfloat16).astype(jnp.float32)
+        )
         spread(n, 1)
         gradient(n, 1, top, n > 0)
         advance(n, 1, top)
@@ -254,7 +326,13 @@
     def _():
         for n in range(samples):
             guess_copy(n).wait_send()
-            corr_copy(n).wait_send()
+            corr_copy(n, cbuf).wait_send()
+        rates_copy.wait_send()
+
+    @pl.when(to_second)
+    def _():
+        for n in range(samples):
+            second_copy(n).wait_send()
 
     out_corr.wait()
     for slot in range(slots):
@@ -293,14 +371,21 @@
             pltpu.VMEM((samples, side, side, chan), bf),
             pltpu.VMEM((samples, side, side, chan), bf),
             pltpu.VMEM((samples, side, side, chan), bf),
+            pltpu.VMEM((samples, side, side, chan), bf),
+            pltpu.VMEM((samples, side, side, chan), bf),
+            pltpu.VMEM((samples, side, side, chan), bf),
+            pltpu.VMEM((samples, side, side, chan), bf),
+            pltpu.VMEM((1, chan), f32),
+            pltpu.VMEM((samples * cells, chan), f32),
             pltpu.VMEM((samples * cells, chan), f32),
             pltpu.VMEM((samples, side + 2, side, 3 * chan), bf),
             pltpu.VMEM((slots, 2, half, chan), f32),
             pltpu.VMEM((slots, half, chan), f32),
             pltpu.VMEM((dps, slots, half, chan), bf),
             pltpu.VMEM((slots, 2, half, chan), bf),
-            dma((3,)),
+            dma((4,)),
             dma((samples,)), dma((samples,)), dma((samples,)), dma((samples,)),
+            dma((samples,)), dma((samples,)), dma((1,)), dma((1,)),
             dma((slots,)), dma((slots,)),
             dma((slots, dps)), dma((slots, dps)),
             dma((slots,)), dma((slots,)),

time: 49.9 us -> 49.2 us (0.986)
  Pallas kernels: 44.3 us -> 43.6 us
    pallas_call x1, Pallas kernels: 44.3 us -> 43.6 us  [per_device(): pl.pallas_call(functools.partial(kernel, sizes), out_shape=(jax.ShapeDtyp...]
where the time goes in v2:
time: 49.2 us; the launch traced here: 49 us
  Pallas kernels  43.6 us (89%)
  local copies, waits for them, and re-layouts  4.08 us (8%)
  between operations  1.29 us (3%)
    pallas_call x1, Pallas kernels, per_device(): pl.pallas_call(functools.partial(kernel, sizes), out_shape=(jax.ShapeDtyp...  43.6 us
    unnamed x2, local copies, waits for them, and re-layouts  4.08 us

profile of v2, /device:TPU:0, one launch (start us, length us, event | category | flops | bytes accessed | tf_op | source)
XLA Modules:
  0.0 49.0 jit_solution(13530484825699195946)
XLA Ops:
  1.3 43.6 %sweep.1 = (bf16[4,16,16,128]{3,2,1,0:T(8,128)(2,1)}, bf16[4,2,576,128]{3,2,1,0:T(8,128)(2,1)}) custom-call(bf16[4,4,16,16,128]{4,3,2,1,0:T(8,128)(2,1)} %bitcast.8, bf16[4,9,128,128]{3,2,1,0:T(8,128)(2,1)} %bitcast.7, bf16[4,16,16,128]{3,2,1,0:T(8,128)(2,1)} %bitcast.9, bf16[4,16,16,128]{3,2,1,0:T(8,128)(2,1)} %term_hbm.1, f32[1,128]{1,0:T(1,128)} %rates_ref.1, ...), custom_call_target="tpu_custom_call" | custom-call | flops 3623878656 | bytes 5000000 | tf_op jit(solution)/shard_map/sweep/pallas_call | solution.py:357
  44.9 1.7 %copy.11 = bf16[1,4,16,16,128]{4,3,2,1,0:T(8,128)(2,1)} copy(bf16[1,4,16,16,128]{4,3,2,1,0:T(8,128)(2,1)} %bitcast.6) | data formatting | bytes 524288
  46.6 2.4 %copy.12 = bf16[1,4,9,128,128]{4,3,2,1,0:T(8,128)(2,1)} copy(bf16[1,4,9,128,128]{4,3,2,1,0:T(8,128)(2,1)} %bitcast.5) | data formatting | bytes 2359296

commit v3 on v2

--- a/solution.py
+++ b/solution.py
@@ -360,7 +360,7 @@
             jax.ShapeDtypeStruct((samples, side, side, chan), bf),
             jax.ShapeDtypeStruct((slots, 2, half, chan), bf),
         ),
-        in_specs=[anywhere] * 4
+        in_specs=[pl.BlockSpec(memory_space=pltpu.HBM)] * 4
         + [pl.BlockSpec(memory_space=pltpu.VMEM), pl.BlockSpec(memory_space=pltpu.SMEM)],
         out_specs=(anywhere, anywhere),
         scratch_shapes=[
@@ -392,11 +392,11 @@
             dma((3, slots)),
         ],
         compiler_params=pltpu.CompilerParams(
-            collective_id=0, has_side_effects=True, vmem_limit_bytes=60 * 1024 * 1024
+            collective_id=0, has_side_effects=True, vmem_limit_bytes=40 * 1024 * 1024
         ),
         cost_estimate=pl.CostEstimate(flops=flops, bytes_accessed=5_000_000, transcendentals=0),
         name="sweep",
-    )(activations[0], weights[0], guesses[0], terminal, coarse_rates, block_layers)
+    )(*[pltpu.with_memory_space_constraint(v, pltpu.HBM) for v in (activations[0], weights[0], guesses[0], terminal)], coarse_rates, block_layers)
     return corrected[None], grads.reshape(1, slots, taps, chan, chan)
 
 

time: 49.2 us -> 46.3 us (0.941)
  local copies, waits for them, and re-layouts: 4.08 us -> 2.37 us
  Pallas kernels: 43.6 us -> 42.4 us
    unnamed x2 -> x4, local copies, waits for them, and re-layouts: 4.08 us -> 2.37 us
    pallas_call x1, Pallas kernels: 43.6 us -> 42.4 us  [per_device(): pl.pallas_call(functools.partial(kernel, sizes), out_shape=(jax.ShapeDtyp...]
where the time goes in v3:
time: 46.3 us; the launch traced here: 46.1 us
  Pallas kernels  42.4 us (92%)
  local copies, waits for them, and re-layouts  2.37 us (5%)
  between operations  1.29 us (3%)
    pallas_call x1, Pallas kernels, per_device(): pl.pallas_call(functools.partial(kernel, sizes), out_shape=(jax.ShapeDtyp...  42.4 us
    unnamed x4, local copies, waits for them, and re-layouts  2.37 us

profile of v3, /device:TPU:0, one launch (start us, length us, event | category | flops | bytes accessed | tf_op | source)
XLA Modules:
  0.0 46.1 jit_solution(7891072643922157149)
XLA Ops:
  1.3 0.0 copy-start
  1.3 0.6 %copy-done = f32[1,128]{1,0:T(1,128)S(1)} copy-done((f32[1,128]{1,0:T(1,128)S(1)}, f32[1,128]{1,0:T(1,128)}, u32[]{:S(2)}) %copy-start) | copy-done | bytes 536
  1.9 42.4 %sweep.1 = (bf16[4,16,16,128]{3,2,1,0:T(8,128)(2,1)S(1)}, bf16[4,2,576,128]{3,2,1,0:T(8,128)(2,1)S(1)}) custom-call(bf16[4,4,16,16,128]{4,3,2,1,0:T(8,128)(2,1)} %bitcast.8, bf16[4,9,128,128]{3,2,1,0:T(8,128)(2,1)} %bitcast.7, bf16[4,16,16,128]{3,2,1,0:T(8,128)(2,1)} %bitcast.9, bf16[4,16,16,128]{3,2,1,0:T(8,128)(2,1)} %term_hbm.1, f32[1,128]{1,0:T(1,128)S(1)} %copy-done, ...), custom_call_target="tpu_custom_call" | custom-call | flops 3623878656 | bytes 5000000 | tf_op jit(solution)/shard_map/sweep/pallas_call | solution.py:357
  44.4 0.7 %copy.11 = bf16[1,4,16,16,128]{4,3,2,1,0:T(8,128)(2,1)} copy(bf16[1,4,16,16,128]{4,3,2,1,0:T(8,128)(2,1)S(1)} %bitcast.6) | data formatting | bytes 524288
  45.1 1.0 %copy.12 = bf16[1,4,9,128,128]{4,3,2,1,0:T(8,128)(2,1)} copy(bf16[1,4,9,128,128]{4,3,2,1,0:T(8,128)(2,1)S(1)} %bitcast.5) | data formatting | bytes 2359296
Async XLA Ops:
  1.3 0.7 %copy-start = (f32[1,128]{1,0:T(1,128)S(1)}, f32[1,128]{1,0:T(1,128)}, u32[]{:S(2)}) copy-start(f32[1,128]{1,0:T(1,128)} %rates_ref.1) | copy-start | bytes 1540

commit v4 on v3

--- a/solution.py
+++ b/solution.py
@@ -13,9 +13,9 @@
 
 def kernel(
     sizes,
-    acts_hbm, w_hbm, guess_hbm, term_hbm, rates_ref, count_ref,
+    acts_hbm, w_hbm, guess_hbm, term_hbm, rates_hbm, count_ref,
     corr_hbm, grads_hbm,
-    acts, w, wt, at, gbuf, rbuf, kbuf, cbuf, pbuf, kout, own, rnext, state, start, shifts, grad, part, xbuf, fin,
+    acts, w, wt, at, gbuf, rbuf, kbuf, cbuf, pbuf, kout, own, rates_ref, rnext, state, start, shifts, grad, part, xbuf, fin,
     local_sem, gsend, grecv, csend, crecv, ksend, krecv, rsend, rrecv, psend, precv, xsend, xrecv, fsend, frecv, out_sem,
 ):
     layers, dps, chans = sizes
@@ -33,6 +33,7 @@
         pltpu.make_async_copy(w_hbm, w, local_sem.at[0]),
         pltpu.make_async_copy(acts_hbm, acts, local_sem.at[1]),
         pltpu.make_async_copy(guess_hbm, own, local_sem.at[3]),
+        pltpu.make_async_copy(rates_hbm, rates_ref, local_sem.at[4]),
     ]
     for load in loads:
         load.start()
@@ -101,7 +102,6 @@
     def _():
         for n in range(early):
             guess_copy(n).start()
-        rates_copy.start()
 
     @pl.when(has_prev & has_next)
     def _():
@@ -112,6 +112,11 @@
     shifts[:, side + 1] = jnp.zeros((samples,) + shifts.shape[2:], shifts.dtype)
     for load in loads:
         load.wait()
+
+    @pl.when(has_prev)
+    def _():
+        rates_copy.start()
+
     for slot in range(slots):
         for tap in range(9):
             wt[slot, tap * chan:(tap + 1) * chan] = w[slot, tap].T
@@ -180,6 +185,9 @@
                     grad[slot, which, place:place + size] = piece
                     done += size
 
+    def skips(n):
+        return n >= 0
+
     def settle(n):
         @pl.when(jnp.logical_not(has_next))
         def _():
@@ -189,24 +197,26 @@
         def _():
             corr_copy(n, cbuf).wait_recv()
 
-        @pl.when(from_second)
-        def _():
-            second_copy(n).wait_recv()
-
         above = rbuf[n].astype(jnp.float32).reshape(cells, chan)
-        term = rnext[...] * kbuf[n].astype(jnp.float32).reshape(cells, chan)
-        above = above + jnp.where(from_second, 1.0, 0.0).astype(jnp.float32) * term
+        if skips(n):
+            @pl.when(from_second)
+            def _():
+                second_copy(n).wait_recv()
+
+            term = rnext[...] * kbuf[n].astype(jnp.float32).reshape(cells, chan)
+            above = above + jnp.where(from_second, 1.0, 0.0).astype(jnp.float32) * term
         later = above - gbuf[n].astype(jnp.float32).reshape(cells, chan)
         whole = prop_of(n) + rates_ref[...] * later
         cbuf[n] = whole.astype(jnp.bfloat16).reshape(side, side, chan)
-        alone = whole - own[n].astype(jnp.float32).reshape(cells, chan)
-        kout[n] = alone.astype(jnp.bfloat16).reshape(side, side, chan)
-
-        @pl.when(to_second)
-        def _():
-            second_copy(n).start()
-
-        @pl.when(has_prev & odd)
+        if skips(n):
+            alone = whole - own[n].astype(jnp.float32).reshape(cells, chan)
+            kout[n] = alone.astype(jnp.bfloat16).reshape(side, side, chan)
+
+            @pl.when(to_second)
+            def _():
+                second_copy(n).start()
+
+        @pl.when(has_prev & odd if skips(n) else has_prev)
         def _():
             corr_copy(n, cbuf).start()
 
@@ -228,11 +238,12 @@
         for slot in reversed(range(slots)):
             spread(n, 1)
             advance(n, 1, slot)
-        pbuf[n] = prop_of(n).astype(jnp.bfloat16).reshape(side, side, chan)
-
-        @pl.when(has_prev & jnp.logical_not(odd))
-        def _():
-            corr_copy(n, pbuf).start()
+        if skips(n):
+            pbuf[n] = prop_of(n).astype(jnp.bfloat16).reshape(side, side, chan)
+
+            @pl.when(has_prev & jnp.logical_not(odd))
+            def _():
+                corr_copy(n, pbuf).start()
 
         if n + early < samples:
             @pl.when(has_prev & jnp.logical_not(has_next))
@@ -245,6 +256,13 @@
                 def _():
                     settle(m)
 
+    def partner_copy(slot):
+        return pltpu.make_async_remote_copy(
+            src_ref=grad.at[slot, 1 - c], dst_ref=part.at[slot],
+            send_sem=psend.at[slot], recv_sem=precv.at[slot],
+            device_id={"chan": 1 - c}, device_id_type=MESH,
+        )
+
     top = slots - 1
     for n in range(samples):
         @pl.when(behind >= samples - 1 - n)
@@ -256,29 +274,32 @@
         )
         spread(n, 1)
         gradient(n, 1, top, n > 0)
+        if n == samples - 1:
+            partner_copy(top).start()
         advance(n, 1, top)
 
     out_corr = pltpu.make_async_copy(cbuf, corr_hbm, out_sem.at[0, 0])
     out_corr.start()
 
-    def partner_copy(slot):
-        return pltpu.make_async_remote_copy(
-            src_ref=grad.at[slot, 1 - c], dst_ref=part.at[slot],
-            send_sem=psend.at[slot], recv_sem=precv.at[slot],
-            device_id={"chan": 1 - c}, device_id_type=MESH,
-        )
-
-    def peer_copy(slot, source, target):
-        return pltpu.make_async_remote_copy(
-            src_ref=xbuf.at[source, slot], dst_ref=xbuf.at[source, slot],
-            send_sem=xsend.at[slot, target], recv_sem=xrecv.at[slot, source],
+    pieces = xsend.shape[1]
+    size = half // pieces
+
+    def rows_of(piece):
+        return pl.ds(piece * size, size)
+
+    def peer_copy(slot, piece, source, target):
+        return pltpu.make_async_remote_copy(
+            src_ref=xbuf.at[source, slot, rows_of(piece)],
+            dst_ref=xbuf.at[source, slot, rows_of(piece)],
+            send_sem=xsend.at[slot, piece, target], recv_sem=xrecv.at[slot, piece, source],
             device_id={"dp": target}, device_id_type=MESH,
         )
 
-    def final_copy(slot, which):
-        return pltpu.make_async_remote_copy(
-            src_ref=fin.at[slot, which], dst_ref=fin.at[slot, which],
-            send_sem=fsend.at[slot], recv_sem=frecv.at[slot],
+    def final_copy(slot, piece, which):
+        return pltpu.make_async_remote_copy(
+            src_ref=fin.at[slot, which, rows_of(piece)],
+            dst_ref=grads_hbm.at[slot, which, rows_of(piece)],
+            send_sem=fsend.at[slot, piece], recv_sem=frecv.at[slot, piece],
             device_id={"chan": 1 - c}, device_id_type=MESH,
         )
 
@@ -289,30 +310,34 @@
 
     def chip_sum(slot):
         partner_copy(slot).wait_recv()
-        xbuf[d, slot] = (grad[slot, c] + part[slot]).astype(jnp.bfloat16)
-        for k in range(1, dps):
-            peer_copy(slot, d, lax.rem(d + k, dps)).start()
+        for piece in range(pieces):
+            rows = rows_of(piece)
+            xbuf[d, slot, rows] = (grad[slot, c, rows] + part[slot, rows]).astype(jnp.bfloat16)
+            for k in range(1, dps):
+                peer_copy(slot, piece, d, lax.rem(d + k, dps)).start()
 
     def finish(slot):
-        for k in range(1, dps):
-            peer_copy(slot, lax.rem(d + k, dps), lax.rem(d + k, dps)).wait_recv()
-        total = xbuf[0, slot].astype(jnp.float32)
-        for e in range(1, dps):
-            total = total + xbuf[e, slot].astype(jnp.float32)
-        fin[slot, c] = total.astype(jnp.bfloat16)
-        final_copy(slot, c).start()
+        for piece in range(pieces):
+            rows = rows_of(piece)
+            for k in range(1, dps):
+                peer = lax.rem(d + k, dps)
+                peer_copy(slot, piece, peer, peer).wait_recv()
+            total = xbuf[0, slot, rows].astype(jnp.float32)
+            for e in range(1, dps):
+                total = total + xbuf[e, slot, rows].astype(jnp.float32)
+            fin[slot, c, rows] = total.astype(jnp.bfloat16)
+            final_copy(slot, piece, c).start()
         out_copy(slot, c, 1).start()
 
     def collect(slot):
-        final_copy(slot, 1 - c).wait_recv()
-        out_copy(slot, 1 - c, 2).start()
-
-    partner_copy(top).start()
+        for piece in range(pieces):
+            final_copy(slot, piece, 1 - c).wait_recv()
+
     for slot in reversed(range(top)):
         spread(0, samples)
+        chip_sum(slot + 1)
         gradient(0, samples, slot, False)
         partner_copy(slot).start()
-        chip_sum(slot + 1)
         if slot:
             advance(0, samples, slot)
     chip_sum(0)
@@ -332,16 +357,17 @@
     @pl.when(to_second)
     def _():
         for n in range(samples):
-            second_copy(n).wait_send()
+            if skips(n):
+                second_copy(n).wait_send()
 
     out_corr.wait()
     for slot in range(slots):
         partner_copy(slot).wait_send()
-        for k in range(1, dps):
-            peer_copy(slot, d, lax.rem(d + k, dps)).wait_send()
-        final_copy(slot, c).wait_send()
+        for piece in range(pieces):
+            for k in range(1, dps):
+                peer_copy(slot, piece, d, lax.rem(d + k, dps)).wait_send()
+            final_copy(slot, piece, c).wait_send()
         out_copy(slot, c, 1).wait()
-        out_copy(slot, 1 - c, 2).wait()
 
 
 def per_device(sizes, activations, weights, guesses, terminal, coarse_rates, block_layers):
@@ -360,8 +386,7 @@
             jax.ShapeDtypeStruct((samples, side, side, chan), bf),
             jax.ShapeDtypeStruct((slots, 2, half, chan), bf),
         ),
-        in_specs=[pl.BlockSpec(memory_space=pltpu.HBM)] * 4
-        + [pl.BlockSpec(memory_space=pltpu.VMEM), pl.BlockSpec(memory_space=pltpu.SMEM)],
+        in_specs=[pl.BlockSpec(memory_space=pltpu.HBM)] * 5 + [pl.BlockSpec(memory_space=pltpu.SMEM)],
         out_specs=(anywhere, anywhere),
         scratch_shapes=[
             pltpu.VMEM((slots, samples, side, side, chan), bf),
@@ -375,6 +400,7 @@
             pltpu.VMEM((samples, side, side, chan), bf),
             pltpu.VMEM((samples, side, side, chan), bf),
             pltpu.VMEM((samples, side, side, chan), bf),
+            pltpu.VMEM((1, chan), f32),
             pltpu.VMEM((1, chan), f32),
             pltpu.VMEM((samples * cells, chan), f32),
             pltpu.VMEM((samples * cells, chan), f32),
@@ -383,12 +409,12 @@
             pltpu.VMEM((slots, half, chan), f32),
             pltpu.VMEM((dps, slots, half, chan), bf),
             pltpu.VMEM((slots, 2, half, chan), bf),
-            dma((4,)),
+            dma((5,)),
             dma((samples,)), dma((samples,)), dma((samples,)), dma((samples,)),
             dma((samples,)), dma((samples,)), dma((1,)), dma((1,)),
             dma((slots,)), dma((slots,)),
-            dma((slots, dps)), dma((slots, dps)),
-            dma((slots,)), dma((slots,)),
+            dma((slots, 2, dps)), dma((slots, 2, dps)),
+            dma((slots, 2)), dma((slots, 2)),
             dma((3, slots)),
         ],
         compiler_params=pltpu.CompilerParams(
@@ -396,7 +422,7 @@
         ),
         cost_estimate=pl.CostEstimate(flops=flops, bytes_accessed=5_000_000, transcendentals=0),
         name="sweep",
-    )(*[pltpu.with_memory_space_constraint(v, pltpu.HBM) for v in (activations[0], weights[0], guesses[0], terminal)], coarse_rates, block_layers)
+    )(*[pltpu.with_memory_space_constraint(v, pltpu.HBM) for v in (activations[0], weights[0], guesses[0], terminal, coarse_rates)], block_layers)
     return corrected[None], grads.reshape(1, slots, taps, chan, chan)
 
 

time: 46.3 us -> 45.8 us (0.989)
  local copies, waits for them, and re-layouts: 2.37 us -> 1.72 us
    unnamed x4 -> x2, local copies, waits for them, and re-layouts: 2.37 us -> 1.72 us
where the time goes in v4:
time: 45.8 us; the launch traced here: 45.7 us
  Pallas kernels  42.7 us (93%)
  local copies, waits for them, and re-layouts  1.72 us (4%)
  between operations  1.29 us (3%)
    pallas_call x1, Pallas kernels, per_device(): pl.pallas_call(functools.partial(kernel, sizes), out_shape=(jax.ShapeDtyp...  42.7 us
    unnamed x2, local copies, waits for them, and re-layouts  1.72 us

profile of v4, /device:TPU:0, one launch (start us, length us, event | category | flops | bytes accessed | tf_op | source)
XLA Modules:
  0.0 45.7 jit_solution(6411837523366106165)
XLA Ops:
  1.3 42.7 %sweep.1 = (bf16[4,16,16,128]{3,2,1,0:T(8,128)(2,1)S(1)}, bf16[4,2,576,128]{3,2,1,0:T(8,128)(2,1)S(1)}) custom-call(bf16[4,4,16,16,128]{4,3,2,1,0:T(8,128)(2,1)} %bitcast.8, bf16[4,9,128,128]{3,2,1,0:T(8,128)(2,1)} %bitcast.7, bf16[4,16,16,128]{3,2,1,0:T(8,128)(2,1)} %bitcast.9, bf16[4,16,16,128]{3,2,1,0:T(8,128)(2,1)} %term_hbm.1, f32[1,128]{1,0:T(1,128)} %rates_hbm.1, ...), custom_call_target="tpu_custom_call" | custom-call | flops 3623878656 | bytes 5000000 | tf_op jit(solution)/shard_map/sweep/pallas_call | solution.py:383
  44.0 0.7 %copy.11 = bf16[1,4,16,16,128]{4,3,2,1,0:T(8,128)(2,1)} copy(bf16[1,4,16,16,128]{4,3,2,1,0:T(8,128)(2,1)S(1)} %bitcast.6) | data formatting | bytes 524288
  44.7 1.0 %copy.12 = bf16[1,4,9,128,128]{4,3,2,1,0:T(8,128)(2,1)} copy(bf16[1,4,9,128,128]{4,3,2,1,0:T(8,128)(2,1)S(1)} %bitcast.5) | data formatting | bytes 2359296
